TPU v7x, 512 devices: a whole 4x4x16 slice. The times are simulated.
512 devices in a mesh: inp: 16 (over z), wgt: 8 (over y_hi, x), out: 4 (over y_lo, core).
Axes of the slice: x: 4, y: 4 (y_hi: 2, y_lo: 2; y = y_hi * 2 + y_lo), z: 16, core: 2. Of those that a mesh axis runs over, the one named last changes fastest.
Arguments:
- tokens: bfloat16 [256, 12288], P(('inp', 'out'), 'wgt'), may hold values from -6 to 6
- in_weight: bfloat16 [12288, 24576], P('wgt', ('inp', 'out')), may hold values from -0.0546875 to 0.0546875
- out_weight: bfloat16 [24576, 12288], P(('inp', 'out'), 'wgt'), may hold values from -0.0390625 to 0.0390625
- grad_output: bfloat16 [256, 12288], P(('inp', 'out'), 'wgt'), may hold values from -3 to 3
Outputs:
- result: bfloat16 [256, 12288], P(('inp', 'out'), 'wgt')
- grad_tokens: bfloat16 [256, 12288], P(('inp', 'out'), 'wgt')
- grad_in_weight: bfloat16 [12288, 24576], P('wgt', ('inp', 'out'))
- grad_out_weight: bfloat16 [24576, 12288], P(('inp', 'out'), 'wgt')
All inputs are finite; a program needn't handle non-finite values.
Results may differ from a plain program's by a relative error of at most 0.024.
Values may be sent and summed in bfloat16 or wider, within the bound.
A program may use at most 64 MiB of HBM per device.

v0:
```python
import math

import jax
import jax.numpy as jnp
from jax import lax
from jax.sharding import PartitionSpec as P

gelu_c = math.sqrt(2.0 / math.pi)


def gelu_value(v):
    inner = jnp.tanh(gelu_c * (v + 0.044715 * v * v * v))
    return 0.5 * v * (1.0 + inner)


def gelu_slope(v):
    inner = jnp.tanh(gelu_c * (v + 0.044715 * v * v * v))
    return 0.5 * (1.0 + inner) + 0.5 * v * (1.0 - inner * inner) * gelu_c * (
        1.0 + 3.0 * 0.044715 * v * v
    )


def on_device(tokens, in_weight, out_weight, grad_output):
    gathered = lax.all_gather(tokens, ("inp", "out"), axis=0, tiled=True)
    preact_part = jnp.dot(gathered, in_weight, preferred_element_type=jnp.float32)
    preact = lax.psum(preact_part.astype(jnp.bfloat16), "wgt").astype(jnp.float32)
    hidden = gelu_value(preact).astype(jnp.bfloat16)
    block = hidden
    result = lax.psum_scatter(
        jnp.dot(block, out_weight, preferred_element_type=jnp.float32),
        ("inp", "out"),
        scatter_dimension=0,
        tiled=True,
    ).astype(jnp.bfloat16)
    cotangent = lax.all_gather(grad_output, ("inp", "out"), axis=0, tiled=True)
    grad_part = lax.dot_general(
        cotangent, out_weight, (((1,), (1,)), ((), ())), preferred_element_type=jnp.float32
    )
    grad_hidden = lax.psum(grad_part.astype(jnp.bfloat16), "wgt").astype(jnp.float32)
    grad_preact = (grad_hidden * gelu_slope(preact)).astype(jnp.bfloat16)
    block = grad_preact
    grad_tokens = lax.psum_scatter(
        lax.dot_general(
            block, in_weight, (((1,), (1,)), ((), ())), preferred_element_type=jnp.float32
        ),
        ("inp", "out"),
        scatter_dimension=0,
        tiled=True,
    ).astype(jnp.bfloat16)
    grad_in_weight = lax.dot_general(
        gathered, grad_preact, (((0,), (0,)), ((), ())), preferred_element_type=jnp.float32
    ).astype(jnp.bfloat16)
    grad_out_weight = lax.dot_general(
        hidden, cotangent, (((0,), (0,)), ((), ())), preferred_element_type=jnp.float32
    ).astype(jnp.bfloat16)
    return (result, grad_tokens, grad_in_weight, grad_out_weight)


def solution(mesh):
    in_specs = (
        P(("inp", "out"), "wgt"),
        P("wgt", ("inp", "out")),
        P(("inp", "out"), "wgt"),
        P(("inp", "out"), "wgt"),
    )
    out_specs = (
        P(("inp", "out"), "wgt"),
        P(("inp", "out"), "wgt"),
        P("wgt", ("inp", "out")),
        P(("inp", "out"), "wgt"),
    )
    return jax.shard_map(
        on_device, mesh=mesh, in_specs=in_specs, out_specs=out_specs, check_vma=False
    )
```

profile of v0, /device:TPU:1, one launch (start us, length us, event | category | flops | bytes accessed | tf_op | source)
XLA Modules:
  0.0 498.4 jit_solution(11797361118008184669)
XLA Ops:
  7.2 0.0 copy-start
  7.2 0.0 all-reduce.7.cloned.1.call-start
  7.2 0.0 copy-start.4
  7.2 73.7 %all-gather.1 = bf16[64,4,1536]{2,1,0:T(4,128)(2,1)S(1)} all-gather(bf16[1,4,1536]{2,1,0:T(4,128)(2,1)} %bitcast.13), channel_id=1, replica_groups=mesh['inp'=16,'wgt'=8,'out'=4] {'inp','out'}, dimensions={0}, use_global_device_ids=true | all-gather | bytes 798720 | tf_op jit(solution)/shard_map/all_gather | solution.py:35
  80.9 0.2 reshape.11
  81.1 0.0 copy-done.4
  81.1 61.7 %all-gather = bf16[64,4,1536]{2,1,0:T(4,128)(2,1)S(1)} all-gather(bf16[1,4,1536]{2,1,0:T(4,128)(2,1)S(1)} %bitcast.14), channel_id=1, replica_groups=mesh['inp'=16,'wgt'=8,'out'=4] {'inp','out'}, dimensions={0}, use_global_device_ids=true | all-gather | bytes 798720 | tf_op jit(solution)/shard_map/all_gather | solution.py:24
  142.8 0.2 reshape.9
  143.0 0.0 copy-done
  143.0 0.0 copy-start.1
  143.0 0.0 copy-start.5
  143.0 1.3 convolution_convert_fusion.2
  144.3 0.3 copy-done.5
  144.6 1.2 convolution_convert_fusion.3
  145.9 0.0 copy-done.1
  145.9 0.0 all-reduce.7.cloned.1.call-update
  145.9 1.3 dynamic-slice
  147.8 88.3 %all-reduce.7.cloned.1.call-done = (bf16[256,384]{1,0:T(8,128)(2,1)}, bf16[256,384]{1,0:T(8,128)(2,1)}) async-done(((bf16[256,384]{1,0:T(8,128)(2,1)}, bf16[256,384]{1,0:T(8,128)(2,1)}), (bf16[256,384]{1,0:T(8,128)(2,1)}, bf16[256,384]{1,0:T(8,128)(2,1)})) %all-reduce.7.cloned.1.call-update) | async-done | bytes 393232 | tf_op jit(solution)/shard_map/psum | solution.py:26
  236.1 0.0 copy-start.3
  236.1 0.0 copy-start.6
  236.1 0.0 copy-start.7
  236.1 1.6 fusion.13
  237.8 0.0 copy-done.3
  237.8 0.0 copy-done.6
  237.8 0.0 copy-done.7
  237.8 0.0 copy-start.2
  237.8 1.9 fusion.16
  239.7 0.0 copy-done.2
  239.7 1.8 fusion
  241.4 1.6 convolution_convert_fusion
  243.0 2.4 copy.9
  245.4 244.8 %all-reduce.8 = (bf16[256,1536]{1,0:T(8,128)(2,1)S(1)}, bf16[256,1536]{1,0:T(8,128)(2,1)}) all-reduce(f32[256,1536]{1,0:T(8,128)S(1)} %fusion.13, f32[256,1536]{1,0:T(8,128)} %fusion.16), channel_id=2, replica_groups=mesh['inp'=16,'wgt'=8,'out'=4] {'inp','out'}, use_global_device_ids=true, to_apply=%region_1.0.clone | all-reduce | flops 786432 | bytes 4718592
  490.2 1.4 dynamic-slice_convert_fusion
Async XLA Ops:
  7.2 135.8 %copy-start = (bf16[384,1536]{1,0:T(8,128)(2,1)S(1)}, bf16[384,1536]{1,0:T(8,128)(2,1)}, u32[]{:S(2)}) copy-start(bf16[384,1536]{1,0:T(8,128)(2,1)} %param.6) | copy-start | bytes 3538948
  7.2 228.9 %all-reduce.7.cloned.1.call-start = ((), (), s32[]{:S(2)}) async-start(), calls=%async_computation | async-start | bytes 786432 | tf_op jit(solution)/shard_map/psum | solution.py:26
  7.2 73.9 %copy-start.4 = (bf16[4,1536]{1,0:T(4,128)(2,1)S(1)}, bf16[4,1536]{1,0:T(4,128)(2,1)}, u32[]{:S(2)}) copy-start(bf16[4,1536]{1,0:T(4,128)(2,1)} %param.4) | copy-start | bytes 36868
  143.0 2.9 copy-start.1
  143.0 1.6 copy-start.5
  236.1 1.6 copy-start.3
  236.1 1.7 copy-start.6
  236.1 1.7 copy-start.7
  237.8 1.9 copy-start.2
Sparse Core Ops, SparseCore 0:
  146.0 90.0 all-reduce.6
where the time goes:
time: 501 us; the launch traced here: 498 us
  blocking collectives  380 us (76%)
  waiting for transfers between devices  88.3 us (18%)
  between operations  14.8 us (3%)
  matrix products  9.35 us (2%)
  local copies, waits for them, and re-layouts  5.72 us (1%)
    unnamed x1, blocking collectives  245 us
    psum x1, waiting for transfers between devices, on_device(): lax.psum(preact_part.astype(jnp.bfloat16), 'wgt').astype(jnp.float32)  88.3 us
    all_gather x1, blocking collectives, on_device(): cotangent = lax.all_gather(grad_output, ('inp', 'out'), axis=0, tiled=True)  73.7 us
    all_gather x1, blocking collectives, on_device(): gathered = lax.all_gather(tokens, ('inp', 'out'), axis=0, tiled=True)  61.7 us
  transfers between devices with their start and end apart: 1, of which 1 were waited for; matrix products, arithmetic and copies ran while one was open for 0% of the time, Pallas kernels for 0%

commit v1 on v0

v1 whole, which is shorter than its diff:
```python
import math

import jax
import jax.numpy as jnp
from jax import lax
from jax.experimental import pallas as pl
from jax.experimental.pallas import tpu as pltpu
from jax.sharding import PartitionSpec as P

MESH = pl.DeviceIdType.MESH
f32 = jnp.float32
bf16 = jnp.bfloat16

gelu_c = math.sqrt(2.0 / math.pi)

FAR = (-6, -2, 2, 6)
NEAR = ((0, 0), (1, 0), (-1, 0), (2, 0), (0, 1), (1, 1), (-1, 1), (-2, 1))
NEAR_ORDER = (7, 5, 6, 3, 4, 1, 2)
PEERS = ((2, 1), (1, 1), (3, 1), (2, 0), (0, 1), (1, 0), (3, 0))


def gelu_value_and_slope(v):
    inner = jnp.tanh(gelu_c * (v + 0.044715 * v * v * v))
    value = 0.5 * v * (1.0 + inner)
    slope = 0.5 * (1.0 + inner) + 0.5 * v * (1.0 - inner * inner) * gelu_c * (
        1.0 + 3.0 * 0.044715 * v * v
    )
    return value, slope


def kernel(
    tok_ref, w1_hbm, w2_hbm, cot_ref,
    res_ref, gt_ref, giw_hbm, gow_hbm,
    w1, w2, giw, gow,
    own, farbuf, stage, rows, part, recva, act, slope,
    keep, sibsend, sibrecv, nearsend, nearrecv, farsend, farrecv,
    load_sem, store_sem,
    far_s, far_r, near_s, near_r, sib_s, sib_r, pa_s, pa_r, pb_s, pb_r,
    rsib_s, rsib_r, rnear_s, rnear_r, rfar_s, rfar_r,
):
    z = lax.axis_index("inp")
    w = lax.axis_index("wgt")
    o = lax.axis_index("out")
    x = w % 4
    yh = w // 4

    def at_z(dz, dy=0):
        return ((z + dz + 16) % 16, w, (o + 2 * dy) % 4)

    sibling = (z, w, o + 1 - 2 * (o % 2))

    def peer_index(k):
        dx, dy = PEERS[k]
        return ((yh + dy) % 2) * 4 + (x + dx) % 4

    load1 = pltpu.make_async_copy(w1_hbm, w1, load_sem.at[0])
    load2 = pltpu.make_async_copy(w2_hbm, w2, load_sem.at[1])
    load1.start()
    load2.start()

    barrier = pltpu.get_barrier_semaphore()
    partners = [at_z(d) for d in (6, -6, 2, -2, 1, -1)]
    partners += [at_z(d, 1) for d in (2, -2, 1, -1, 0)]
    partners += [(z, peer_index(k), o) for k in range(7)]
    partners += [sibling]
    for partner in partners:
        pl.semaphore_signal(barrier, inc=1, device_id=partner, device_id_type=MESH)
    own[0] = tok_ref[...]
    own[1] = cot_ref[...]
    pl.semaphore_wait(barrier, len(partners))

    def remote(src, dst, send, recv, device):
        return pltpu.make_async_remote_copy(
            src_ref=src, dst_ref=dst, send_sem=send, recv_sem=recv,
            device_id=device, device_id_type=MESH,
        )

    def far_copy(t, j):
        return remote(own.at[t], farbuf.at[t, j], far_s.at[t, j], far_r.at[t, j], at_z(-FAR[j]))

    def near_copy(t, m):
        dz, dy = NEAR[m]
        return remote(
            rows.at[t, 0, 0], rows.at[t, 0, m], near_s.at[t, m], near_r.at[t, m], at_z(-dz, dy)
        )

    def sib_copy(t, m):
        return remote(rows.at[t, 0, m], rows.at[t, 1, m], sib_s.at[t, m], sib_r.at[t, m], sibling)

    def pa_copy(t, k):
        p = peer_index(k)
        return remote(part.at[t, p], recva.at[t, k], pa_s.at[t, k], pa_r.at[t, k], (z, p, o))

    def pb_copy(t, k):
        return remote(
            act.at[t, w], act.at[t, w], pb_s.at[t, k], pb_r.at[t, k], (z, peer_index(k), o)
        )

    def rsib_copy(t, m):
        return remote(
            sibsend.at[t, m], sibrecv.at[t, m], rsib_s.at[t, m], rsib_r.at[t, m], sibling
        )

    def rnear_copy(t, m):
        dz, dy = NEAR[m]
        return remote(
            nearsend.at[t, m], nearrecv.at[t, m], rnear_s.at[t, m], rnear_r.at[t, m], at_z(dz, dy)
        )

    def rfar_copy(t, j):
        return remote(
            farsend.at[t, j], farrecv.at[t, j], rfar_s.at[t, j], rfar_r.at[t, j], at_z(FAR[j])
        )

    for t in range(2):
        for j in (0, 3, 1, 2):
            far_copy(t, j).start()
    for t in range(2):
        for j in (1, 2, 0, 3):
            far_copy(t, j).wait_recv()
            stage[t, 4 * j : 4 * j + 4, :] = farbuf[t, j].astype(f32)
        rows[t, 0, 0] = stage[t].astype(bf16)
        for m in NEAR_ORDER:
            near_copy(t, m).start()
        sib_copy(t, 0).start()

    for t in range(2):
        for m in reversed(NEAR_ORDER):
            near_copy(t, m).wait_recv()
            sib_copy(t, m).start()
        for m in range(8):
            sib_copy(t, m).wait_recv()
        (load1, load2)[t].wait()
        gathered = rows[t].reshape(256, 1536)
        if t == 0:
            product = jnp.dot(gathered, w1[...], preferred_element_type=f32)
        else:
            product = lax.dot_general(
                gathered, w2[...], (((1,), (1,)), ((), ())), preferred_element_type=f32
            )
        part[t] = product.astype(bf16).reshape(8, 32, 384)
        for k in range(7):
            pa_copy(t, k).start()

    for t in range(2):
        total = part[t, w].astype(f32)
        for k in reversed(range(7)):
            pa_copy(t, k).wait_recv()
            total = total + recva[t, k].astype(f32)
        if t == 0:
            value, slope_value = gelu_value_and_slope(total)
            slope[...] = slope_value
        else:
            value = total * slope[...]
        act[t, w] = value.astype(bf16)
        for k in range(7):
            pb_copy(t, k).start()

    for t in range(2):
        for k in reversed(range(7)):
            pb_copy(t, k).wait_recv()
        block = act.at[t]

        def column_tile(i, carry, t=t, block=block):
            at = pl.ds(pl.multiple_of(i * 256, 256), 256)
            left = block[...].reshape(256, 384)
            if t == 0:
                product = jnp.dot(left, w2[:, at], preferred_element_type=f32)
            else:
                product = lax.dot_general(
                    left, w1[at, :], (((1,), (1,)), ((), ())), preferred_element_type=f32
                )
            keep[t, :, :, at] = product[:128].reshape(8, 16, 256)
            sibsend[t, :, :, at] = product[128:].astype(bf16).reshape(8, 16, 256)
            return carry

        lax.fori_loop(0, 6, column_tile, 0)
        for m in NEAR_ORDER + (0,):
            rsib_copy(t, m).start()
        for m in NEAR_ORDER:
            rsib_copy(t, m).wait_recv()
            nearsend[t, m] = (keep[t, m] + sibrecv[t, m].astype(f32)).astype(bf16)
            rnear_copy(t, m).start()

    def gow_tile(i, carry):
        at = pl.ds(pl.multiple_of(i * 256, 256), 256)
        right = rows[1, :, :, :, at].reshape(256, 256)
        gow[:, at] = lax.dot_general(
            act[0].reshape(256, 384), right, (((0,), (0,)), ((), ())), preferred_element_type=f32
        ).astype(bf16)
        return carry

    lax.fori_loop(0, 6, gow_tile, 0)
    store2 = pltpu.make_async_copy(gow, gow_hbm, store_sem.at[1])
    store2.start()

    def giw_tile(i, carry):
        at = pl.ds(pl.multiple_of(i * 256, 256), 256)
        left = rows[0, :, :, :, at].reshape(256, 256)
        giw[at, :] = lax.dot_general(
            left, act[1].reshape(256, 384), (((0,), (0,)), ((), ())), preferred_element_type=f32
        ).astype(bf16)
        return carry

    lax.fori_loop(0, 6, giw_tile, 0)
    store1 = pltpu.make_async_copy(giw, giw_hbm, store_sem.at[0])
    store1.start()

    for t in range(2):
        rsib_copy(t, 0).wait_recv()
        total = keep[t, 0] + sibrecv[t, 0].astype(f32)
        for m in reversed(NEAR_ORDER):
            rnear_copy(t, m).wait_recv()
            total = total + nearrecv[t, m].astype(f32)
        stage[t] = total
        for j in (0, 3, 1, 2):
            farsend[t, j] = stage[t, 4 * j : 4 * j + 4, :].astype(bf16)
            rfar_copy(t, j).start()
    for t in range(2):
        total = jnp.zeros((4, 1536), f32)
        for j in (1, 2, 0, 3):
            rfar_copy(t, j).wait_recv()
            total = total + farrecv[t, j].astype(f32)
        (res_ref, gt_ref)[t][...] = total.astype(bf16)

    for t in range(2):
        for j in range(4):
            far_copy(t, j).wait_send()
            rfar_copy(t, j).wait_send()
        for m in NEAR_ORDER:
            near_copy(t, m).wait_send()
            rnear_copy(t, m).wait_send()
        for m in range(8):
            sib_copy(t, m).wait_send()
            rsib_copy(t, m).wait_send()
        for k in range(7):
            pa_copy(t, k).wait_send()
            pb_copy(t, k).wait_send()
    store2.wait()
    store1.wait()


def on_device(tokens, in_weight, out_weight, grad_output):
    vmem = pl.BlockSpec(memory_space=pltpu.VMEM)
    hbm = pl.BlockSpec(memory_space=pl.ANY)
    dma = pltpu.SemaphoreType.DMA
    return pl.pallas_call(
        kernel,
        out_shape=(
            jax.ShapeDtypeStruct((4, 1536), bf16),
            jax.ShapeDtypeStruct((4, 1536), bf16),
            jax.ShapeDtypeStruct((1536, 384), bf16),
            jax.ShapeDtypeStruct((384, 1536), bf16),
        ),
        in_specs=[vmem, hbm, hbm, vmem],
        out_specs=(vmem, vmem, hbm, hbm),
        scratch_shapes=[
            pltpu.VMEM((1536, 384), bf16),
            pltpu.VMEM((384, 1536), bf16),
            pltpu.VMEM((1536, 384), bf16),
            pltpu.VMEM((384, 1536), bf16),
            pltpu.VMEM((2, 4, 1536), bf16),
            pltpu.VMEM((2, 4, 4, 1536), bf16),
            pltpu.VMEM((2, 16, 1536), f32),
            pltpu.VMEM((2, 2, 8, 16, 1536), bf16),
            pltpu.VMEM((2, 8, 32, 384), bf16),
            pltpu.VMEM((2, 7, 32, 384), bf16),
            pltpu.VMEM((2, 8, 32, 384), bf16),
            pltpu.VMEM((32, 384), f32),
            pltpu.VMEM((2, 8, 16, 1536), f32),
            pltpu.VMEM((2, 8, 16, 1536), bf16),
            pltpu.VMEM((2, 8, 16, 1536), bf16),
            pltpu.VMEM((2, 8, 16, 1536), bf16),
            pltpu.VMEM((2, 8, 16, 1536), bf16),
            pltpu.VMEM((2, 4, 4, 1536), bf16),
            pltpu.VMEM((2, 4, 4, 1536), bf16),
            dma((2,)),
            dma((2,)),
        ]
        + [dma((2, n)) for n in (4, 4, 8, 8, 8, 8, 7, 7, 7, 7, 8, 8, 8, 8, 4, 4)],
        compiler_params=pltpu.CompilerParams(
            collective_id=0, has_side_effects=True, vmem_limit_bytes=40 * 2**20
        ),
        cost_estimate=pl.CostEstimate(
            flops=12 * 256 * 1536 * 384, bytes_accessed=4 * 1536 * 384 * 2, transcendentals=32 * 384
        ),
    )(tokens, in_weight, out_weight, grad_output)


def solution(mesh):
    in_specs = (
        P(("inp", "out"), "wgt"),
        P("wgt", ("inp", "out")),
        P(("inp", "out"), "wgt"),
        P(("inp", "out"), "wgt"),
    )
    out_specs = (
        P(("inp", "out"), "wgt"),
        P(("inp", "out"), "wgt"),
        P("wgt", ("inp", "out")),
        P(("inp", "out"), "wgt"),
    )
    return jax.shard_map(
        on_device, mesh=mesh, in_specs=in_specs, out_specs=out_specs, check_vma=False
    )
```

time: 501 us -> 71.7 us (0.14)
  blocking collectives: 380 us -> 0 us
  waiting for transfers between devices: 88.3 us -> 0 us
  Pallas kernels: 0 us -> 63.6 us
  between operations: 14.8 us -> 0.65 us
  matrix products: 9.35 us -> 0 us
    unnamed x1 -> x0, blocking collectives: 245 us -> none
    all_gather x2 -> x0, blocking collectives: 135 us -> none  [the longest x1 73.7 us: on_device(): cotangent = lax.all_gather(grad_output, ('inp', 'out'), axis=0, tiled=True)]
    psum x1 -> x0, waiting for transfers between devices: 88.3 us -> none  [on_device(): lax.psum(preact_part.astype(jnp.bfloat16), 'wgt').astype(jnp.float32)]
    pallas_call x0 -> x1, Pallas kernels: none -> 63.6 us  [on_device(): pl.pallas_call(kernel, out_shape=(jax.ShapeDtypeStruct((4, 1536), bf16),...]
    dot_general x6 -> x0, matrix products: 9.35 us -> none  [the longest x1 1.87 us: on_device(): lax.dot_general(block, in_weight, (((1,), (1,)), ((), ())), preferred_ele...]
  transfers between devices with their start and end apart: 1 -> 0, of which waited for: 1 -> 0; matrix products, arithmetic and copies ran while one was open for 0% -> 0% of each run, Pallas kernels for 0% -> 0%
where the time goes in v1:
time: 71.7 us; the launch traced here: 71.5 us
  Pallas kernels  63.6 us (89%)
  local copies, waits for them, and re-layouts  7.17 us (10%)
    pallas_call x1, Pallas kernels, on_device(): pl.pallas_call(kernel, out_shape=(jax.ShapeDtypeStruct((4, 1536), bf16),...  63.6 us
    unnamed x12, local copies, waits for them, and re-layouts  7.17 us

profile of v1, /device:TPU:1, one launch (start us, length us, event | category | flops | bytes accessed | tf_op | source)
XLA Modules:
  0.0 71.5 jit_solution(15496229279160889567)
XLA Ops:
  0.6 0.0 copy-start
  0.6 1.3 %copy-done = bf16[1536,384]{1,0:T(8,128)(2,1)S(1)} copy-done((bf16[1536,384]{1,0:T(8,128)(2,1)S(1)}, bf16[1536,384]{1,0:T(8,128)(2,1)}, u32[]{:S(2)}) %copy-start) | copy-done | bytes 1179672
  1.9 0.0 copy-start.1
  1.9 1.3 %copy-done.1 = bf16[384,1536]{1,0:T(8,128)(2,1)S(1)} copy-done((bf16[384,1536]{1,0:T(8,128)(2,1)S(1)}, bf16[384,1536]{1,0:T(8,128)(2,1)}, u32[]{:S(2)}) %copy-start.1) | copy-done | bytes 1179672
  3.2 0.0 copy-start.2
  3.2 0.7 copy-done.2
  3.9 0.0 copy-start.3
  3.9 0.7 copy-done.3
  4.6 63.6 %shard_map.75 = (bf16[4,1536]{1,0:T(4,128)(2,1)S(1)}, bf16[4,1536]{1,0:T(4,128)(2,1)S(1)}, bf16[1536,384]{1,0:T(8,128)(2,1)S(1)}, bf16[384,1536]{1,0:T(8,128)(2,1)S(1)}) custom-call(bf16[4,1536]{1,0:T(4,128)(2,1)S(1)} %copy-done.2, bf16[1536,384]{1,0:T(8,128)(2,1)S(1)} %copy-done, bf16[384,1536]{1,0:T(8,128)(2,1)S(1)} %copy-done.1, bf16[4,1536]{1,0:T(4,128)(2,1)S(1)} %copy-done.3), custom_call_target="tpu_custom_call" | custom-call | flops 1811939328 | bytes 4718592 | tf_op jit(solution)/shard_map/pallas_call | solution.py:247
  68.2 0.6 copy.12
  68.8 0.6 copy.13
  69.4 1.0 %copy.14 = bf16[1536,384]{1,0:T(8,128)(2,1)} copy(bf16[1536,384]{1,0:T(8,128)(2,1)S(1)} %get-tuple-element.10) | data formatting | bytes 2359296
  70.4 1.0 %copy.15 = bf16[384,1536]{1,0:T(8,128)(2,1)} copy(bf16[384,1536]{1,0:T(8,128)(2,1)S(1)} %get-tuple-element.11) | data formatting | bytes 2359296
Async XLA Ops:
  0.6 1.3 %copy-start = (bf16[1536,384]{1,0:T(8,128)(2,1)S(1)}, bf16[1536,384]{1,0:T(8,128)(2,1)}, u32[]{:S(2)}) copy-start(bf16[1536,384]{1,0:T(8,128)(2,1)} %w1_hbm.1) | copy-start | bytes 3538948
  1.9 1.3 %copy-start.1 = (bf16[384,1536]{1,0:T(8,128)(2,1)S(1)}, bf16[384,1536]{1,0:T(8,128)(2,1)}, u32[]{:S(2)}) copy-start(bf16[384,1536]{1,0:T(8,128)(2,1)} %w2_hbm.1) | copy-start | bytes 3538948
  3.2 0.7 copy-start.2
  3.9 0.7 copy-start.3

commit v2 on v1

v2 whole, which is shorter than its diff:
```python
import math

import jax
import jax.numpy as jnp
from jax import lax
from jax.experimental import pallas as pl
from jax.experimental.pallas import tpu as pltpu
from jax.sharding import PartitionSpec as P

MESH = pl.DeviceIdType.MESH
f32 = jnp.float32
bf16 = jnp.bfloat16

gelu_c = math.sqrt(2.0 / math.pi)

FAR = (-6, -2, 2, 6)
NEAR = ((0, 0), (1, 0), (-1, 0), (2, 0), (0, 1), (1, 1), (-1, 1), (-2, 1))
NEAR_ORDER = (7, 5, 6, 3, 4, 1, 2)
PEERS = ((2, 1), (1, 1), (3, 1), (2, 0), (0, 1), (1, 0), (3, 0))


def gelu_value_and_slope(v):
    inner = jnp.tanh(gelu_c * (v + 0.044715 * v * v * v))
    value = 0.5 * v * (1.0 + inner)
    slope = 0.5 * (1.0 + inner) + 0.5 * v * (1.0 - inner * inner) * gelu_c * (
        1.0 + 3.0 * 0.044715 * v * v
    )
    return value, slope


def kernel(
    tok_hbm, w1_hbm, w2_hbm, cot_hbm,
    res_ref, gt_ref, giw, gow,
    w1, w2, w1t, w2t,
    own, farbuf, stage, rows, part, recva, act, shared, slope,
    keep, nearsend, nearrecv, farsend, farrecv,
    load_sem, weight_s, weight_r, rows_s, rows_r, shared_s, shared_r,
    far_s, far_r, near_s, near_r, pa_s, pa_r, pb_s, pb_r,
    rnear_s, rnear_r, rfar_s, rfar_r,
):
    z = lax.axis_index("inp")
    w = lax.axis_index("wgt")
    o = lax.axis_index("out")
    x = w % 4
    yh = w // 4

    def at_z(dz, dy=0):
        return ((z + dz + 16) % 16, w, (o + 2 * dy) % 4)

    sibling = (z, w, o + 1 - 2 * (o % 2))

    def peer_index(k):
        dx, dy = PEERS[k]
        return ((yh + dy) % 2) * 4 + (x + dx) % 4

    loads = [
        pltpu.make_async_copy(src, dst, load_sem.at[i])
        for i, (src, dst) in enumerate(
            (
                (tok_hbm, own.at[0]),
                (cot_hbm, own.at[1]),
                (w2_hbm, w2.at[pl.ds(0, 384)]),
                (w1_hbm, w1.at[:, pl.ds(0, 384)]),
            )
        )
    ]
    for load in loads:
        load.start()

    barrier = pltpu.get_barrier_semaphore()
    partners = [at_z(d) for d in (6, -6, 2, -2, 1, -1)]
    partners += [at_z(d, 1) for d in (2, -2, 1, -1, 0)]
    partners += [(z, peer_index(k), o) for k in range(7)]
    partners += [sibling]
    for partner in partners:
        pl.semaphore_signal(barrier, inc=1, device_id=partner, device_id_type=MESH)
    loads[0].wait()
    loads[1].wait()
    pl.semaphore_wait(barrier, len(partners))

    def remote(src, dst, send, recv, device):
        return pltpu.make_async_remote_copy(
            src_ref=src, dst_ref=dst, send_sem=send, recv_sem=recv,
            device_id=device, device_id_type=MESH,
        )

    sent = []

    def start(copy):
        copy.start()
        sent.append(copy)

    def far_copy(t, j):
        return remote(own.at[t], farbuf.at[t, j], far_s.at[t, j], far_r.at[t, j], at_z(-FAR[j]))

    def near_copy(t, m):
        dz, dy = NEAR[m]
        return remote(
            rows.at[t, 0, 0], rows.at[t, 0, m], near_s.at[t, m], near_r.at[t, m], at_z(-dz, dy)
        )

    def rows_copy(t):
        return remote(rows.at[t, 0], rows.at[t, 1], rows_s.at[t], rows_r.at[t], sibling)

    def shared_copy(t):
        return remote(
            act.at[t, :, :, pl.ds(384, 384)], shared.at[t, 1], shared_s.at[t], shared_r.at[t],
            sibling,
        )

    def pa_copy(t, k):
        p = peer_index(k)
        return remote(part.at[t, p], recva.at[t, k], pa_s.at[t, k], pa_r.at[t, k], (z, p, o))

    def pb_copy(t, k):
        return remote(
            act.at[t, w], act.at[t, w], pb_s.at[t, k], pb_r.at[t, k], (z, peer_index(k), o)
        )

    def rnear_copy(t, m):
        dz, dy = NEAR[m]
        return remote(
            nearsend.at[t, m], nearrecv.at[t, m], rnear_s.at[t, m], rnear_r.at[t, m], at_z(dz, dy)
        )

    def rfar_copy(t, j):
        return remote(
            farsend.at[t, j], farrecv.at[t, j], rfar_s.at[t, j], rfar_r.at[t, j], at_z(FAR[j])
        )

    for t in range(2):
        for j in (0, 3, 1, 2):
            start(far_copy(t, j))
    weights = (
        remote(w2_hbm, w2.at[pl.ds(384, 384)], weight_s.at[0], weight_r.at[0], sibling),
        remote(w1_hbm, w1.at[:, pl.ds(384, 384)], weight_s.at[1], weight_r.at[1], sibling),
    )
    for copy in weights:
        start(copy)
    loads[2].wait()
    weights[0].wait_recv()
    w2t[...] = w2[...].T
    for t in range(2):
        for j in (1, 2, 0, 3):
            far_copy(t, j).wait_recv()
            stage[t, 4 * j : 4 * j + 4, :] = farbuf[t, j].astype(f32)
        rows[t, 0, 0] = stage[t].astype(bf16)
        for m in NEAR_ORDER:
            start(near_copy(t, m))
    loads[3].wait()
    weights[1].wait_recv()
    w1t[...] = w1[...].T

    for t in range(2):
        for m in reversed(NEAR_ORDER):
            near_copy(t, m).wait_recv()
        part[t] = (
            jnp.dot(
                rows[t, 0].reshape(128, 1536), (w1, w2t)[t][...], preferred_element_type=f32
            )
            .astype(bf16)
            .reshape(8, 16, 768)
        )
        for k in range(7):
            start(pa_copy(t, k))
        start(rows_copy(t))

    for t in range(2):
        total = part[t, w].astype(f32)
        for k in reversed(range(7)):
            pa_copy(t, k).wait_recv()
            total = total + recva[t, k].astype(f32)
        if t == 0:
            value, slope_value = gelu_value_and_slope(total)
            slope[...] = slope_value
        else:
            value = total * slope[...]
        act[t, w] = value.astype(bf16)
        for k in range(7):
            start(pb_copy(t, k))

    for t in range(2):
        for k in reversed(range(7)):
            pb_copy(t, k).wait_recv()
        product = jnp.dot(
            act[t].reshape(128, 768), (w2, w1t)[t][...], preferred_element_type=f32
        ).reshape(8, 16, 1536)
        nearsend[t] = product.astype(bf16)
        keep[t] = product[0]
        for m in NEAR_ORDER:
            start(rnear_copy(t, m))
        start(shared_copy(t))
        shared[t, 0] = act[t, :, :, :384]

    for t in range(2):
        rows_copy(1 - t).wait_recv()
        shared_copy(t).wait_recv()
        units = shared[t].reshape(256, 384)
        other = rows[1 - t].reshape(256, 1536)
        if t == 0:
            gow[...] = lax.dot_general(
                units, other, (((0,), (0,)), ((), ())), preferred_element_type=f32
            ).astype(bf16)
        else:
            giw[...] = lax.dot_general(
                other, units, (((0,), (0,)), ((), ())), preferred_element_type=f32
            ).astype(bf16)

    for t in range(2):
        total = keep[t]
        for m in reversed(NEAR_ORDER):
            rnear_copy(t, m).wait_recv()
            total = total + nearrecv[t, m].astype(f32)
        stage[t] = total
        for j in (0, 3, 1, 2):
            farsend[t, j] = stage[t, 4 * j : 4 * j + 4, :].astype(bf16)
            start(rfar_copy(t, j))
    for t in range(2):
        total = jnp.zeros((4, 1536), f32)
        for j in (1, 2, 0, 3):
            rfar_copy(t, j).wait_recv()
            total = total + farrecv[t, j].astype(f32)
        (res_ref, gt_ref)[t][...] = total.astype(bf16)

    for copy in sent:
        copy.wait_send()


def store_kernel(*refs):
    sem = refs[8]
    stores = [pltpu.make_async_copy(refs[i], refs[4 + i], sem.at[i]) for i in (2, 3, 0, 1)]
    for store in stores:
        store.start()
    for store in stores:
        store.wait()


def on_device(*arguments):
    vmem = pl.BlockSpec(memory_space=pltpu.VMEM)
    hbm = pl.BlockSpec(memory_space=pltpu.HBM)
    dma = pltpu.SemaphoreType.DMA
    out_shape = (
        jax.ShapeDtypeStruct((4, 1536), bf16),
        jax.ShapeDtypeStruct((4, 1536), bf16),
        jax.ShapeDtypeStruct((1536, 384), bf16),
        jax.ShapeDtypeStruct((384, 1536), bf16),
    )
    outputs = pl.pallas_call(
        kernel,
        out_shape=out_shape,
        in_specs=[hbm] * 4,
        out_specs=(vmem,) * 4,
        scratch_shapes=[
            pltpu.VMEM((1536, 768), bf16),
            pltpu.VMEM((768, 1536), bf16),
            pltpu.VMEM((768, 1536), bf16),
            pltpu.VMEM((1536, 768), bf16),
            pltpu.VMEM((2, 4, 1536), bf16),
            pltpu.VMEM((2, 4, 4, 1536), bf16),
            pltpu.VMEM((2, 16, 1536), f32),
            pltpu.VMEM((2, 2, 8, 16, 1536), bf16),
            pltpu.VMEM((2, 8, 16, 768), bf16),
            pltpu.VMEM((2, 7, 16, 768), bf16),
            pltpu.VMEM((2, 8, 16, 768), bf16),
            pltpu.VMEM((2, 2, 8, 16, 384), bf16),
            pltpu.VMEM((16, 768), f32),
            pltpu.VMEM((2, 16, 1536), f32),
            pltpu.VMEM((2, 8, 16, 1536), bf16),
            pltpu.VMEM((2, 8, 16, 1536), bf16),
            pltpu.VMEM((2, 4, 4, 1536), bf16),
            pltpu.VMEM((2, 4, 4, 1536), bf16),
            dma((4,)),
        ]
        + [dma((2,))] * 6
        + [dma((2, n)) for n in (4, 4, 8, 8, 7, 7, 7, 7, 8, 8, 4, 4)],
        compiler_params=pltpu.CompilerParams(
            collective_id=0, has_side_effects=True, vmem_limit_bytes=40 * 2**20
        ),
        cost_estimate=pl.CostEstimate(
            flops=12 * 256 * 1536 * 384, bytes_accessed=4 * 1536 * 384 * 2, transcendentals=32 * 384
        ),
    )(*(pltpu.with_memory_space_constraint(a, pltpu.HBM) for a in arguments))
    return pl.pallas_call(
        store_kernel,
        out_shape=out_shape,
        in_specs=[vmem] * 4,
        out_specs=(hbm,) * 4,
        scratch_shapes=[dma((4,))],
        compiler_params=pltpu.CompilerParams(vmem_limit_bytes=8 * 2**20),
    )(*outputs)


def solution(mesh):
    in_specs = (
        P(("inp", "out"), "wgt"),
        P("wgt", ("inp", "out")),
        P(("inp", "out"), "wgt"),
        P(("inp", "out"), "wgt"),
    )
    out_specs = (
        P(("inp", "out"), "wgt"),
        P(("inp", "out"), "wgt"),
        P("wgt", ("inp", "out")),
        P(("inp", "out"), "wgt"),
    )
    return jax.shard_map(
        on_device, mesh=mesh, in_specs=in_specs, out_specs=out_specs, check_vma=False
    )
```

time: 71.7 us -> 65.9 us (0.919)
  the two profiles are of different devices: /device:TPU:1 before, /device:TPU:18 now
where the time goes in v2:
time: 65.9 us; the launch traced here: 65.7 us
  Pallas kernels  65 us (99%)
    pallas_call x1, Pallas kernels, on_device(): pl.pallas_call(kernel, out_shape=out_shape, in_specs=[hbm] * 4, out_specs...  63.6 us
    pallas_call x1, Pallas kernels, on_device(): pl.pallas_call(store_kernel, out_shape=out_shape, in_specs=[vmem] * 4, ou...  1.44 us

profile of v2, /device:TPU:18, one launch (start us, length us, event | category | flops | bytes accessed | tf_op | source)
XLA Modules:
  0.0 65.7 jit_solution(10031659990963359753)
XLA Ops:
  0.6 63.6 %shard_map.75 = (bf16[4,1536]{1,0:T(4,128)(2,1)S(1)}, bf16[4,1536]{1,0:T(4,128)(2,1)S(1)}, bf16[1536,384]{1,0:T(8,128)(2,1)S(1)}, bf16[384,1536]{1,0:T(8,128)(2,1)S(1)}) custom-call(bf16[4,1536]{1,0:T(4,128)(2,1)} %tok_hbm.1, bf16[1536,384]{1,0:T(8,128)(2,1)} %w1_hbm.1, bf16[384,1536]{1,0:T(8,128)(2,1)} %w2_hbm.1, bf16[4,1536]{1,0:T(4,128)(2,1)} %cot_hbm.1), custom_call_target="tpu_custom_call" | custom-call | flops 1811939328 | bytes 4718592 | tf_op jit(solution)/shard_map/pallas_call | solution.py:248
  64.2 1.4 %shard_map.76 = (bf16[4,1536]{1,0:T(4,128)(2,1)}, bf16[4,1536]{1,0:T(4,128)(2,1)}, bf16[1536,384]{1,0:T(8,128)(2,1)}, bf16[384,1536]{1,0:T(8,128)(2,1)}) custom-call(bf16[4,1536]{1,0:T(4,128)(2,1)S(1)} %get-tuple-element.8.refs_0_, bf16[4,1536]{1,0:T(4,128)(2,1)S(1)} %get-tuple-element.9.refs_1_, bf16[1536,384]{1,0:T(8,128)(2,1)S(1)} %get-tuple-element.10.refs_2_, ...), custom_call_target="tpu_custom_call" | custom-call | tf_op jit(solution)/shard_map/pallas_call | solution.py:283

commit v3 on v2

--- a/solution.py
+++ b/solution.py
@@ -13,9 +13,13 @@
 
 gelu_c = math.sqrt(2.0 / math.pi)
 
-FAR = (-6, -2, 2, 6)
+FAR = (-2, -6, 6, 2)
+FAR_ORDER = (1, 2, 0, 3)
 NEAR = ((0, 0), (1, 0), (-1, 0), (2, 0), (0, 1), (1, 1), (-1, 1), (-2, 1))
 NEAR_ORDER = (7, 5, 6, 3, 4, 1, 2)
+SPAN = (None, (1, 4), (0, 3), (1, 4), (1, 3), (1, 4), (0, 3), (0, 3))
+DIRECT = ((4, 0), (4, 3), (5, 0), (6, 3), (1, 0), (2, 3), (7, 3))
+HOME = (3, 0)
 PEERS = ((2, 1), (1, 1), (3, 1), (2, 0), (0, 1), (1, 0), (3, 0))
 
 
@@ -32,11 +36,11 @@
     tok_hbm, w1_hbm, w2_hbm, cot_hbm,
     res_ref, gt_ref, giw, gow,
     w1, w2, w1t, w2t,
-    own, farbuf, stage, rows, part, recva, act, shared, slope,
-    keep, nearsend, nearrecv, farsend, farrecv,
+    own, blocks, stage, rows, part, recva, act, shared, slope,
+    keep, back, nearrecv, directrecv, farsend, farrecv,
     load_sem, weight_s, weight_r, rows_s, rows_r, shared_s, shared_r,
     far_s, far_r, near_s, near_r, pa_s, pa_r, pb_s, pb_r,
-    rnear_s, rnear_r, rfar_s, rfar_r,
+    rnear_s, rnear_r, rfar_s, rfar_r, direct_s, direct_r, rdirect_s, rdirect_r,
 ):
     z = lax.axis_index("inp")
     w = lax.axis_index("wgt")
@@ -91,12 +95,22 @@
         sent.append(copy)
 
     def far_copy(t, j):
-        return remote(own.at[t], farbuf.at[t, j], far_s.at[t, j], far_r.at[t, j], at_z(-FAR[j]))
+        return remote(own.at[t], blocks.at[t, 0, j], far_s.at[t, j], far_r.at[t, j], at_z(-FAR[j]))
+
+    def direct_copy(t, i):
+        m, j = DIRECT[i]
+        dz, dy = NEAR[m]
+        return remote(
+            own.at[t], blocks.at[t, m, j], direct_s.at[t, i], direct_r.at[t, i],
+            at_z(-dz - FAR[j], dy),
+        )
 
     def near_copy(t, m):
         dz, dy = NEAR[m]
-        return remote(
-            rows.at[t, 0, 0], rows.at[t, 0, m], near_s.at[t, m], near_r.at[t, m], at_z(-dz, dy)
+        span = pl.ds(SPAN[m][0], SPAN[m][1] - SPAN[m][0])
+        return remote(
+            blocks.at[t, 0, span], blocks.at[t, m, span], near_s.at[t, m], near_r.at[t, m],
+            at_z(-dz, dy),
         )
 
     def rows_copy(t):
@@ -117,10 +131,20 @@
             act.at[t, w], act.at[t, w], pb_s.at[t, k], pb_r.at[t, k], (z, peer_index(k), o)
         )
 
+    def rdirect_copy(t, i):
+        m, j = DIRECT[i]
+        dz, dy = NEAR[m]
+        return remote(
+            back.at[t, m, j], directrecv.at[t, i], rdirect_s.at[t, i], rdirect_r.at[t, i],
+            at_z(dz + FAR[j], dy),
+        )
+
     def rnear_copy(t, m):
         dz, dy = NEAR[m]
-        return remote(
-            nearsend.at[t, m], nearrecv.at[t, m], rnear_s.at[t, m], rnear_r.at[t, m], at_z(dz, dy)
+        span = pl.ds(SPAN[m][0], SPAN[m][1] - SPAN[m][0])
+        return remote(
+            back.at[t, m, span], nearrecv.at[t, m, span], rnear_s.at[t, m], rnear_r.at[t, m],
+            at_z(dz, dy),
         )
 
     def rfar_copy(t, j):
@@ -129,31 +153,44 @@
         )
 
     for t in range(2):
-        for j in (0, 3, 1, 2):
+        for j in FAR_ORDER:
             start(far_copy(t, j))
+    for t in range(2):
+        for i in range(7):
+            start(direct_copy(t, i))
     weights = (
         remote(w2_hbm, w2.at[pl.ds(384, 384)], weight_s.at[0], weight_r.at[0], sibling),
         remote(w1_hbm, w1.at[:, pl.ds(384, 384)], weight_s.at[1], weight_r.at[1], sibling),
     )
     for copy in weights:
         start(copy)
+    for t in range(2):
+        blocks[t, HOME[0], HOME[1]] = own[t]
     loads[2].wait()
     weights[0].wait_recv()
     w2t[...] = w2[...].T
-    for t in range(2):
-        for j in (1, 2, 0, 3):
+
+    def to_rows(t, m):
+        for j in range(4):
+            stage[t, 4 * j : 4 * j + 4, :] = blocks[t, m, j].astype(f32)
+        rows[t, 0, m] = stage[t].astype(bf16)
+
+    for t in range(2):
+        for j in reversed(FAR_ORDER):
             far_copy(t, j).wait_recv()
-            stage[t, 4 * j : 4 * j + 4, :] = farbuf[t, j].astype(f32)
-        rows[t, 0, 0] = stage[t].astype(bf16)
         for m in NEAR_ORDER:
             start(near_copy(t, m))
+        to_rows(t, 0)
     loads[3].wait()
     weights[1].wait_recv()
     w1t[...] = w1[...].T
 
     for t in range(2):
+        for i in range(7):
+            direct_copy(t, i).wait_recv()
         for m in reversed(NEAR_ORDER):
             near_copy(t, m).wait_recv()
+            to_rows(t, m)
         part[t] = (
             jnp.dot(
                 rows[t, 0].reshape(128, 1536), (w1, w2t)[t][...], preferred_element_type=f32
@@ -185,12 +222,31 @@
         product = jnp.dot(
             act[t].reshape(128, 768), (w2, w1t)[t][...], preferred_element_type=f32
         ).reshape(8, 16, 1536)
-        nearsend[t] = product.astype(bf16)
-        keep[t] = product[0]
+        keep[t] = product
+
+        def to_back(m, j, t=t):
+            back[t, m, j] = keep[t, m, 4 * j : 4 * j + 4, :].astype(bf16)
+
         for m in NEAR_ORDER:
+            for j in range(*SPAN[m]):
+                to_back(m, j)
             start(rnear_copy(t, m))
+        for i in range(7):
+            to_back(*DIRECT[i])
+            start(rdirect_copy(t, i))
         start(shared_copy(t))
         shared[t, 0] = act[t, :, :, :384]
+
+    for t in range(2):
+        for m in reversed(NEAR_ORDER):
+            rnear_copy(t, m).wait_recv()
+        for j in FAR_ORDER:
+            total = keep[t, 0, 4 * j : 4 * j + 4, :]
+            for m in NEAR_ORDER:
+                if SPAN[m][0] <= j < SPAN[m][1]:
+                    total = total + nearrecv[t, m, j].astype(f32)
+            farsend[t, j] = total.astype(bf16)
+            start(rfar_copy(t, j))
 
     for t in range(2):
         rows_copy(1 - t).wait_recv()
@@ -207,17 +263,11 @@
             ).astype(bf16)
 
     for t in range(2):
-        total = keep[t]
-        for m in reversed(NEAR_ORDER):
-            rnear_copy(t, m).wait_recv()
-            total = total + nearrecv[t, m].astype(f32)
-        stage[t] = total
-        for j in (0, 3, 1, 2):
-            farsend[t, j] = stage[t, 4 * j : 4 * j + 4, :].astype(bf16)
-            start(rfar_copy(t, j))
-    for t in range(2):
-        total = jnp.zeros((4, 1536), f32)
-        for j in (1, 2, 0, 3):
+        total = keep[t, HOME[0], 4 * HOME[1] : 4 * HOME[1] + 4, :]
+        for i in range(7):
+            rdirect_copy(t, i).wait_recv()
+            total = total + directrecv[t, i].astype(f32)
+        for j in reversed(FAR_ORDER):
             rfar_copy(t, j).wait_recv()
             total = total + farrecv[t, j].astype(f32)
         (res_ref, gt_ref)[t][...] = total.astype(bf16)
@@ -226,9 +276,12 @@
         copy.wait_send()
 
 
-def store_kernel(*refs):
-    sem = refs[8]
-    stores = [pltpu.make_async_copy(refs[i], refs[4 + i], sem.at[i]) for i in (2, 3, 0, 1)]
+def store_kernel(res, gt, giw, gow, res_hbm, gt_hbm, giw_hbm, gow_hbm, sem):
+    pieces = [(res, res_hbm), (gt, gt_hbm)]
+    for i in range(4):
+        for src, dst, n in ((giw, giw_hbm, 384), (gow, gow_hbm, 96)):
+            pieces.append((src.at[pl.ds(i * n, n)], dst.at[pl.ds(i * n, n)]))
+    stores = [pltpu.make_async_copy(*piece, sem.at[i]) for i, piece in enumerate(pieces)]
     for store in stores:
         store.start()
     for store in stores:
@@ -256,7 +309,7 @@
             pltpu.VMEM((768, 1536), bf16),
             pltpu.VMEM((1536, 768), bf16),
             pltpu.VMEM((2, 4, 1536), bf16),
-            pltpu.VMEM((2, 4, 4, 1536), bf16),
+            pltpu.VMEM((2, 8, 4, 4, 1536), bf16),
             pltpu.VMEM((2, 16, 1536), f32),
             pltpu.VMEM((2, 2, 8, 16, 1536), bf16),
             pltpu.VMEM((2, 8, 16, 768), bf16),
@@ -264,15 +317,16 @@
             pltpu.VMEM((2, 8, 16, 768), bf16),
             pltpu.VMEM((2, 2, 8, 16, 384), bf16),
             pltpu.VMEM((16, 768), f32),
-            pltpu.VMEM((2, 16, 1536), f32),
-            pltpu.VMEM((2, 8, 16, 1536), bf16),
-            pltpu.VMEM((2, 8, 16, 1536), bf16),
+            pltpu.VMEM((2, 8, 16, 1536), f32),
+            pltpu.VMEM((2, 8, 4, 4, 1536), bf16),
+            pltpu.VMEM((2, 8, 4, 4, 1536), bf16),
+            pltpu.VMEM((2, 7, 4, 1536), bf16),
             pltpu.VMEM((2, 4, 4, 1536), bf16),
             pltpu.VMEM((2, 4, 4, 1536), bf16),
             dma((4,)),
         ]
         + [dma((2,))] * 6
-        + [dma((2, n)) for n in (4, 4, 8, 8, 7, 7, 7, 7, 8, 8, 4, 4)],
+        + [dma((2, n)) for n in (4, 4, 8, 8, 7, 7, 7, 7, 8, 8, 4, 4, 7, 7, 7, 7)],
         compiler_params=pltpu.CompilerParams(
             collective_id=0, has_side_effects=True, vmem_limit_bytes=40 * 2**20
         ),
@@ -285,7 +339,7 @@
         out_shape=out_shape,
         in_specs=[vmem] * 4,
         out_specs=(hbm,) * 4,
-        scratch_shapes=[dma((4,))],
+        scratch_shapes=[dma((10,))],
         compiler_params=pltpu.CompilerParams(vmem_limit_bytes=8 * 2**20),
     )(*outputs)
 

time: 65.9 us -> 62.4 us (0.947)
  the two profiles are of different devices: /device:TPU:18 before, /device:TPU:32 now
where the time goes in v3:
time: 62.4 us; the launch traced here: 62.2 us
  Pallas kernels  61.6 us (99%)
  between operations  0.64 us (1%)
    pallas_call x1, Pallas kernels, on_device(): pl.pallas_call(kernel, out_shape=out_shape, in_specs=[hbm] * 4, out_specs...  60.1 us
    pallas_call x1, Pallas kernels, on_device(): pl.pallas_call(store_kernel, out_shape=out_shape, in_specs=[vmem] * 4, ou...  1.49 us

profile of v3, /device:TPU:32, one launch (start us, length us, event | category | flops | bytes accessed | tf_op | source)
XLA Modules:
  0.0 62.2 jit_solution(18013315881652414601)
XLA Ops:
  0.6 60.1 %shard_map.75 = (bf16[4,1536]{1,0:T(4,128)(2,1)S(1)}, bf16[4,1536]{1,0:T(4,128)(2,1)S(1)}, bf16[1536,384]{1,0:T(8,128)(2,1)S(1)}, bf16[384,1536]{1,0:T(8,128)(2,1)S(1)}) custom-call(bf16[4,1536]{1,0:T(4,128)(2,1)} %tok_hbm.1, bf16[1536,384]{1,0:T(8,128)(2,1)} %w1_hbm.1, bf16[384,1536]{1,0:T(8,128)(2,1)} %w2_hbm.1, bf16[4,1536]{1,0:T(4,128)(2,1)} %cot_hbm.1), custom_call_target="tpu_custom_call" | custom-call | flops 1811939328 | bytes 4718592 | tf_op jit(solution)/shard_map/pallas_call | solution.py:301
  60.7 1.5 %shard_map.76 = (bf16[4,1536]{1,0:T(4,128)(2,1)}, bf16[4,1536]{1,0:T(4,128)(2,1)}, bf16[1536,384]{1,0:T(8,128)(2,1)}, bf16[384,1536]{1,0:T(8,128)(2,1)}) custom-call(bf16[4,1536]{1,0:T(4,128)(2,1)S(1)} %get-tuple-element.8.res, bf16[4,1536]{1,0:T(4,128)(2,1)S(1)} %get-tuple-element.9.gt, bf16[1536,384]{1,0:T(8,128)(2,1)S(1)} %get-tuple-element.10.giw, ...), custom_call_target="tpu_custom_call" | custom-call | tf_op jit(solution)/shard_map/pallas_call | solution.py:337

commit v4 on v3

--- a/solution.py
+++ b/solution.py
@@ -48,10 +48,11 @@
     x = w % 4
     yh = w // 4
 
+    mate = o + 1 - 2 * (o % 2)
+    sibling = (z, w, mate)
+
     def at_z(dz, dy=0):
-        return ((z + dz + 16) % 16, w, (o + 2 * dy) % 4)
-
-    sibling = (z, w, o + 1 - 2 * (o % 2))
+        return ((z + dz + 16) % 16, w, (mate + 2 * dy) % 4)
 
     def peer_index(k):
         dx, dy = PEERS[k]

time: 62.4 us -> 59.8 us (0.958)
  the two profiles are of different devices: /device:TPU:32 before, /device:TPU:1 now
where the time goes in v4:
time: 59.8 us; the launch traced here: 59.3 us
  Pallas kernels  58.7 us (98%)
  between operations  0.64 us (1%)
    pallas_call x1, Pallas kernels, on_device(): pl.pallas_call(kernel, out_shape=out_shape, in_specs=[hbm] * 4, out_specs...  57.2 us
    pallas_call x1, Pallas kernels, on_device(): pl.pallas_call(store_kernel, out_shape=out_shape, in_specs=[vmem] * 4, ou...  1.49 us

profile of v4, /device:TPU:1, one launch (start us, length us, event | category | flops | bytes accessed | tf_op | source)
XLA Modules:
  0.0 59.3 jit_solution(11724138183733416133)
XLA Ops:
  0.6 57.2 %shard_map.75 = (bf16[4,1536]{1,0:T(4,128)(2,1)S(1)}, bf16[4,1536]{1,0:T(4,128)(2,1)S(1)}, bf16[1536,384]{1,0:T(8,128)(2,1)S(1)}, bf16[384,1536]{1,0:T(8,128)(2,1)S(1)}) custom-call(bf16[4,1536]{1,0:T(4,128)(2,1)} %tok_hbm.1, bf16[1536,384]{1,0:T(8,128)(2,1)} %w1_hbm.1, bf16[384,1536]{1,0:T(8,128)(2,1)} %w2_hbm.1, bf16[4,1536]{1,0:T(4,128)(2,1)} %cot_hbm.1), custom_call_target="tpu_custom_call" | custom-call | flops 1811939328 | bytes 4718592 | tf_op jit(solution)/shard_map/pallas_call | solution.py:302
  57.8 1.5 %shard_map.76 = (bf16[4,1536]{1,0:T(4,128)(2,1)}, bf16[4,1536]{1,0:T(4,128)(2,1)}, bf16[1536,384]{1,0:T(8,128)(2,1)}, bf16[384,1536]{1,0:T(8,128)(2,1)}) custom-call(bf16[4,1536]{1,0:T(4,128)(2,1)S(1)} %get-tuple-element.8.res, bf16[4,1536]{1,0:T(4,128)(2,1)S(1)} %get-tuple-element.9.gt, bf16[1536,384]{1,0:T(8,128)(2,1)S(1)} %get-tuple-element.10.giw, ...), custom_call_target="tpu_custom_call" | custom-call | tf_op jit(solution)/shard_map/pallas_call | solution.py:338
